TPU v7x, 32 devices: a whole 2x2x4 slice. The times are simulated.
32 devices in a mesh: groups: 2 (over y), gx: 8 (over z, x), gy: 2 (over core).
Axes of the slice: x: 2, y: 2, z: 4, core: 2. Of those that a mesh axis runs over, the one named last changes fastest.
Arguments:
- tokens: bfloat16 [64, 8192], P(('groups', 'gx'), 'gy'), parts along dimension 0, may hold values from -6 to 6
- gate_weight: bfloat16 [3584, 8192], P('gx', 'gy'), may hold values from -0.0625 to 0.0625
- up_weight: bfloat16 [3584, 8192], P('gx', 'gy'), may hold values from -0.0625 to 0.0625
- down_weight: bfloat16 [3584, 8192], P('gx', 'gy'), may hold values from -0.125 to 0.125
Outputs:
- stream: bfloat16 [64, 8192], P(('groups', 'gx'), 'gy'), parts along dimension 0
There are 2 independent parts, one for each index of `groups`. A program takes and returns all parts, laid end to end along the dimension named above; an argument that names none is the same for every part. Nothing has to cross between parts.
All inputs are finite; a program needn't handle non-finite values.
Results may differ from a plain program's by a relative error of at most 0.0075.
Values may be sent and summed in bfloat16 or wider, within the bound.
A program may use at most 64 MiB of HBM per device.

v0:
```python
import jax
import jax.numpy as jnp
from jax import lax
from jax.sharding import PartitionSpec as P

LAYERS = 2


def local(tokens, gate_weight, up_weight, down_weight):
    stream = tokens
    units = gate_weight.shape[0]
    contract = (((1,), (1,)), ((), ()))
    for repeat in range(LAYERS):
        block_rows = lax.all_gather(stream, "gx", axis=0, tiled=True)
        gate_rows = lax.dot_general(
            block_rows, gate_weight, contract, preferred_element_type=jnp.float32
        )
        up_rows = lax.dot_general(
            block_rows, up_weight, contract, preferred_element_type=jnp.float32
        )
        joined = jnp.concatenate([gate_rows, up_rows], axis=1)
        gate_part = joined[:, :units]
        up_part = joined[:, units:]
        gate_share, up_share = (
            lax.psum_scatter(gate_part, "gy", scatter_dimension=1, tiled=True),
            lax.psum_scatter(up_part, "gy", scatter_dimension=1, tiled=True),
        )
        hidden_share = (jax.nn.silu(gate_share) * up_share).astype(jnp.bfloat16)
        hidden = lax.all_gather(hidden_share, "gy", axis=1, tiled=True)
        partial_value = jnp.dot(hidden, down_weight, preferred_element_type=jnp.float32)
        summed = lax.psum_scatter(partial_value, "gx", scatter_dimension=0, tiled=True)
        stream = (stream.astype(jnp.float32) + summed).astype(jnp.bfloat16)
    return stream


def solution(mesh):
    return jax.shard_map(
        local,
        mesh=mesh,
        in_specs=(P(("groups", "gx"), "gy"), P("gx", "gy"), P("gx", "gy"), P("gx", "gy")),
        out_specs=P(("groups", "gx"), "gy"),
        check_vma=False,
    )
```

profile of v0, /device:TPU:0, one launch (start us, length us, event | category | flops | bytes accessed | tf_op | source)
XLA Modules:
  0.0 285.5 jit_solution(13044079156367850146)
XLA Ops:
  6.5 0.0 reduce-scatter.13.cloned.1.call-start
  6.5 32.7 %all-gather = bf16[8,4,4096]{2,1,0:T(4,128)(2,1)S(1)} all-gather(bf16[1,4,4096]{2,1,0:T(4,128)(2,1)} %bitcast.40), channel_id=1, replica_groups=mesh['groups'=2,'gx'=8,'gy'=2] {'gx'}, dimensions={0}, use_global_device_ids=true | all-gather | bytes 294912 | tf_op jit(solution)/shard_map/all_gather | solution.py:14
  39.3 0.1 reshape.1
  39.3 3.8 %convolution_bitcast_fusion.3 = f32[448,32]{1,0:T(8,128)} fusion(bf16[32,4096]{1,0:T(8,128)(2,1)S(1)} %reshape.1, bf16[448,4096]{1,0:T(8,128)(2,1)} %param.5), kind=kOutput, calls=%fused_computation.3 | convolution fusion | flops 117440512 | bytes 3989504
  43.2 0.0 reduce-scatter.13.cloned.1.call-update
  43.2 0.0 reduce-scatter.15.cloned.1.call-start
  43.2 3.8 %convolution_bitcast_fusion.2 = f32[448,32]{1,0:T(8,128)} fusion(bf16[32,4096]{1,0:T(8,128)(2,1)S(1)} %reshape.1, bf16[448,4096]{1,0:T(8,128)(2,1)} %param.6), kind=kOutput, calls=%fused_computation.2 | convolution fusion | flops 117440512 | bytes 3989504
  47.1 0.0 copy-start.1
  47.1 0.0 copy-start
  47.1 0.0 reduce-scatter.15.cloned.1.call-update
  47.1 0.0 all-reduce.5.cloned.1.call-start
  47.1 4.8 %reduce-scatter.13.cloned.1.call-done = f32[224,32]{1,0:T(8,128)} async-done(((f32[448,32]{1,0:T(8,128)}), f32[224,32]{1,0:T(8,128)}) %reduce-scatter.13.cloned.1.call-update) | async-done | bytes 28688
  51.9 1.0 copy.10
  52.9 10.1 %reduce-scatter.15.cloned.1.call-done = f32[224,32]{1,0:T(8,128)} async-done(((f32[448,32]{1,0:T(8,128)}), f32[224,32]{1,0:T(8,128)}) %reduce-scatter.15.cloned.1.call-update) | async-done | bytes 28688
  62.9 1.0 copy.12
  63.9 1.8 all-gather.1
  65.8 0.1 reshape.3
  65.9 3.6 %fusion.5 = f32[32,4096]{1,0:T(8,128)} fusion(bf16[448,32]{0,1:T(8,128)(2,1)S(1)} %reshape.3, bf16[448,4096]{1,0:T(8,128)(2,1)} %param.7), kind=kOutput, calls=%fused_computation.13 | convolution fusion | flops 117440512 | bytes 4222976 | tf_op jit(solution)/shard_map/dot_general | solution.py:30
  69.5 0.0 all-reduce.5.cloned.1.call-update
  69.5 0.0 reduce-scatter.17.cloned.1.call-start
  69.6 0.0 copy-done.1
  69.6 0.6 dynamic-slice
  70.8 72.3 %all-reduce.5.cloned.1.call-done = f32[32,4096]{1,0:T(8,128)} async-done(((f32[32,4096]{1,0:T(8,128)}), f32[32,4096]{1,0:T(8,128)}) %all-reduce.5.cloned.1.call-update) | async-done | bytes 524304
  143.1 0.0 copy-done
  143.1 0.9 fusion.4
  144.1 30.9 %all-gather.2 = bf16[8,4,4096]{2,1,0:T(4,128)(2,1)S(1)} all-gather(bf16[1,4,4096]{2,1,0:T(4,128)(2,1)S(1)} %fusion.4), channel_id=1, replica_groups=mesh['groups'=2,'gx'=8,'gy'=2] {'gx'}, dimensions={0}, use_global_device_ids=true | all-gather | bytes 294912 | tf_op jit(solution)/shard_map/all_gather | solution.py:14
  175.0 0.1 reshape.5
  175.0 3.8 %convolution_bitcast_fusion.1 = f32[448,32]{1,0:T(8,128)} fusion(bf16[32,4096]{1,0:T(8,128)(2,1)S(1)} %reshape.5, bf16[448,4096]{1,0:T(8,128)(2,1)} %param.5), kind=kOutput, calls=%fused_computation.1 | convolution fusion | flops 117440512 | bytes 3989504
  178.9 0.0 reduce-scatter.17.cloned.1.call-update
  178.9 0.0 reduce-scatter.19.cloned.1.call-start
  178.9 3.8 %convolution_bitcast_fusion = f32[448,32]{1,0:T(8,128)} fusion(bf16[32,4096]{1,0:T(8,128)(2,1)S(1)} %reshape.5, bf16[448,4096]{1,0:T(8,128)(2,1)} %param.6), kind=kOutput, calls=%fused_computation | convolution fusion | flops 117440512 | bytes 3989504
  182.8 0.0 reduce-scatter.19.cloned.1.call-update
  182.8 0.0 all-reduce.7.cloned.1.call-start
  182.8 3.0 %reduce-scatter.17.cloned.1.call-done = f32[224,32]{1,0:T(8,128)} async-done(((f32[448,32]{1,0:T(8,128)}), f32[224,32]{1,0:T(8,128)}) %reduce-scatter.17.cloned.1.call-update) | async-done | bytes 28688
  185.8 1.0 copy.14
  186.8 10.0 %reduce-scatter.19.cloned.1.call-done = f32[224,32]{1,0:T(8,128)} async-done(((f32[448,32]{1,0:T(8,128)}), f32[224,32]{1,0:T(8,128)}) %reduce-scatter.19.cloned.1.call-update) | async-done | bytes 28688
  196.8 1.0 copy.16
  197.8 1.8 all-gather.3
  199.6 0.1 reshape.7
  199.7 3.6 %fusion.6 = f32[32,4096]{1,0:T(8,128)} fusion(bf16[448,32]{0,1:T(8,128)(2,1)S(1)} %reshape.7, bf16[448,4096]{1,0:T(8,128)(2,1)} %param.7), kind=kOutput, calls=%fused_computation.14 | convolution fusion | flops 117440512 | bytes 4222976 | tf_op jit(solution)/shard_map/dot_general | solution.py:30
  203.3 0.0 all-reduce.7.cloned.1.call-update
  203.4 73.7 %all-reduce.7.cloned.1.call-done = f32[32,4096]{1,0:T(8,128)} async-done(((f32[32,4096]{1,0:T(8,128)}), f32[32,4096]{1,0:T(8,128)}) %all-reduce.7.cloned.1.call-update) | async-done | bytes 524304
  277.1 1.6 fusion
  (4 shorter events, 0.1 us)
Async XLA Ops:
  6.5 45.4 %reduce-scatter.13.cloned.1.call-start = ((), (), s32[]{:S(2)}) async-start(), calls=%async_computation.4 | async-start | bytes 344064
  43.2 19.7 %reduce-scatter.15.cloned.1.call-start = ((), (), s32[]{:S(2)}) async-start(), calls=%async_computation.5 | async-start | bytes 344064
  47.1 22.5 %copy-start.1 = (u32[32]{0:T(128)S(1)}, u32[32]{0:T(128)}, u32[]{:S(2)}) copy-start(u32[32]{0:T(128)} %constant.7) | copy-start | bytes 388
  47.1 96.1 %copy-start = (bf16[4,4096]{1,0:T(4,128)(2,1)S(1)}, bf16[4,4096]{1,0:T(4,128)(2,1)}, u32[]{:S(2)}) copy-start(bf16[4,4096]{1,0:T(4,128)(2,1)} %param.4) | copy-start | bytes 98308
  47.1 96.0 %all-reduce.5.cloned.1.call-start = ((), (), s32[]{:S(2)}) async-start(), calls=%async_computation.8 | async-start | bytes 1048576
  69.5 116.3 %reduce-scatter.17.cloned.1.call-start = ((), (), s32[]{:S(2)}) async-start(), calls=%async_computation.6 | async-start | bytes 344064
  178.9 17.9 %reduce-scatter.19.cloned.1.call-start = ((), (), s32[]{:S(2)}) async-start(), calls=%async_computation.7 | async-start | bytes 344064
  182.8 94.3 %all-reduce.7.cloned.1.call-start = ((), (), s32[]{:S(2)}) async-start(), calls=%async_computation.9 | async-start | bytes 1048576
Sparse Core Ops, SparseCore 0:
  43.3 8.5 reduce-scatter.12
  54.2 8.7 reduce-scatter.14
  69.6 73.4 all-reduce.4
  179.0 6.7 reduce-scatter.16
  188.0 8.7 reduce-scatter.18
  203.5 73.5 all-reduce.6
where the time goes:
time: 286 us
  waiting for transfers between devices  174 us (61%)
  blocking collectives  67.3 us (24%)
  matrix products  22.5 us (8%)
  between operations  14.2 us (5%)
  local copies, waits for them, and re-layouts  4.81 us (2%)
    unnamed x12, waiting for transfers between devices  174 us
    all_gather x2, blocking collectives, local(): block_rows = lax.all_gather(stream, 'gx', axis=0, tiled=True)  63.6 us
    unnamed x4, matrix products  15.3 us
    dot_general x2, matrix products, local(): jnp.dot(hidden, down_weight, preferred_element_type=jnp.float32)  7.2 us
  transfers between devices with their start and end apart: 6, of which 6 were waited for; matrix products, arithmetic and copies ran while one was open for 4% of the time, Pallas kernels for 0%

commit v1 on v0

v1 whole, which is shorter than its diff:
```python
import functools

import jax
import jax.numpy as jnp
from jax import lax
from jax.experimental import pallas as pl
from jax.experimental.pallas import tpu as pltpu
from jax.sharding import PartitionSpec as P

LAYERS = 2
CHUNKS = 4
MESH = pl.DeviceIdType.MESH
F32 = jnp.float32
BF16 = jnp.bfloat16
NT = (((1,), (1,)), ((), ()))


def kernel(n, tokens, wg_hbm, wu_hbm, wd_hbm, out,
           wg, wu, wd, ag, snd, rcv, part, part_in,
           w_sem, tok_sem, ag_send, ag_recv, rs_send, rs_recv, gy_send, gy_recv):
    me = lax.axis_index("gx")
    my_gy = lax.axis_index("gy")
    other = 1 - my_gy
    r, d = tokens.shape
    kc = d // CHUNKS
    rows = n * r

    def cols(c):
        return pl.ds(c * kc, kc)

    loads = []
    for c in range(CHUNKS):
        t = pltpu.make_async_copy(tokens.at[:, cols(c)], ag.at[0, c, me], tok_sem.at[c])
        t.start()
        loads.append(t)
    weights = {}
    for k, (h, v) in enumerate(((wg_hbm, wg), (wu_hbm, wu), (wd_hbm, wd))):
        for c in range(CHUNKS):
            weights[k, c] = pltpu.make_async_copy(h.at[:, cols(c)], v.at[c], w_sem.at[k, c])
    for c in range(CHUNKS):
        weights[0, c].start()
        weights[1, c].start()
    for c in range(CHUNKS):
        weights[2, c].start()

    barrier = pltpu.get_barrier_semaphore()

    def greet(i, carry):
        pl.semaphore_signal(barrier, inc=1, device_id={"gx": lax.rem(me + i, n)}, device_id_type=MESH)
        return carry

    unroll = n <= 8
    lax.fori_loop(1, n, greet, 0, unroll=unroll)
    pl.semaphore_signal(barrier, inc=1, device_id={"gy": other}, device_id_type=MESH)
    for t in loads:
        t.wait()
    pl.semaphore_wait(barrier, n)

    def send_ag(l, c):
        def body(i, carry):
            pltpu.make_async_remote_copy(
                src_ref=ag.at[l, c, me], dst_ref=ag.at[l, c, me],
                send_sem=ag_send.at[l], recv_sem=ag_recv.at[l, c],
                device_id={"gx": lax.rem(me + i, n)}, device_id_type=MESH).start()
            return carry
        lax.fori_loop(1, n, body, 0, unroll=unroll)

    def send_rs(l, c):
        def body(i, carry):
            peer = lax.rem(me + i, n)
            pltpu.make_async_remote_copy(
                src_ref=snd.at[l, c, peer], dst_ref=rcv.at[l, c, me],
                send_sem=rs_send.at[l], recv_sem=rs_recv.at[l, c],
                device_id={"gx": peer}, device_id_type=MESH).start()
            return carry
        lax.fori_loop(1, n, body, 0, unroll=unroll)

    def arrived(buf, sem):
        pltpu.make_async_copy(buf, buf, sem).wait()

    for c in range(CHUNKS):
        send_ag(0, c)

    for l in range(LAYERS):
        gate = up = None
        for c in range(CHUNKS):
            if l == 0:
                weights[0, c].wait()
                weights[1, c].wait()
            arrived(ag.at[l, c, pl.ds(0, n - 1)], ag_recv.at[l, c])
            x = ag[l, c].astype(F32).reshape(rows, kc).astype(BF16)
            g = lax.dot_general(x, wg[c], NT, preferred_element_type=F32)
            u = lax.dot_general(x, wu[c], NT, preferred_element_type=F32)
            gate = g if gate is None else gate + g
            up = u if up is None else up + u
        part[l, 0] = gate
        part[l, 1] = up
        swap = pltpu.make_async_remote_copy(
            src_ref=part.at[l], dst_ref=part_in.at[l],
            send_sem=gy_send.at[l], recv_sem=gy_recv.at[l],
            device_id={"gy": other}, device_id_type=MESH)
        swap.start()
        if l == 0:
            for c in range(CHUNKS):
                weights[2, c].wait()
        swap.wait()
        gate = part[l, 0] + part_in[l, 0]
        up = part[l, 1] + part_in[l, 1]
        hidden = (jax.nn.silu(gate) * up).astype(BF16)
        for c in range(CHUNKS):
            p = jnp.dot(hidden, wd[c], preferred_element_type=F32)
            snd[l, c] = p.reshape(n, r, kc).astype(BF16)
            send_rs(l, c)
            rcv[l, c, me] = snd[l, c, me]
        for c in range(CHUNKS):
            arrived(rcv.at[l, c, pl.ds(0, n - 1)], rs_recv.at[l, c])
            summed = jnp.sum(rcv[l, c].astype(F32), axis=0)
            stream = (ag[l, c, me].astype(F32) + summed).astype(BF16)
            if l + 1 < LAYERS:
                ag[l + 1, c, me] = stream
                send_ag(l + 1, c)
            else:
                out[:, cols(c)] = stream
    for l in range(LAYERS):
        arrived(ag.at[l, :, pl.ds(0, n - 1)], ag_send.at[l])
        arrived(snd.at[l, :, pl.ds(0, n - 1)], rs_send.at[l])


def local(n, tokens, gate_weight, up_weight, down_weight):
    r, d = tokens.shape
    units = gate_weight.shape[0]
    rows = n * r
    kc = d // CHUNKS
    flops = 2 * LAYERS * 3 * rows * units * d
    return pl.pallas_call(
        functools.partial(kernel, n),
        out_shape=jax.ShapeDtypeStruct((r, d), BF16),
        in_specs=[pl.BlockSpec(memory_space=pl.ANY)] * 4,
        out_specs=pl.BlockSpec(memory_space=pltpu.VMEM),
        scratch_shapes=[
            pltpu.VMEM((CHUNKS, units, kc), BF16),
            pltpu.VMEM((CHUNKS, units, kc), BF16),
            pltpu.VMEM((CHUNKS, units, kc), BF16),
            pltpu.VMEM((LAYERS, CHUNKS, n, r, kc), BF16),
            pltpu.VMEM((LAYERS, CHUNKS, n, r, kc), BF16),
            pltpu.VMEM((LAYERS, CHUNKS, n, r, kc), BF16),
            pltpu.VMEM((LAYERS, 2, rows, units), F32),
            pltpu.VMEM((LAYERS, 2, rows, units), F32),
            pltpu.SemaphoreType.DMA((3, CHUNKS)),
            pltpu.SemaphoreType.DMA((CHUNKS,)),
            pltpu.SemaphoreType.DMA((LAYERS,)),
            pltpu.SemaphoreType.DMA((LAYERS, CHUNKS)),
            pltpu.SemaphoreType.DMA((LAYERS,)),
            pltpu.SemaphoreType.DMA((LAYERS, CHUNKS)),
            pltpu.SemaphoreType.DMA((LAYERS,)),
            pltpu.SemaphoreType.DMA((LAYERS,)),
        ],
        compiler_params=pltpu.CompilerParams(
            collective_id=0, has_side_effects=True, vmem_limit_bytes=56 * 1024 * 1024),
        cost_estimate=pl.CostEstimate(
            flops=flops, bytes_accessed=3 * units * d * 2, transcendentals=LAYERS * rows * units),
    )(tokens, gate_weight, up_weight, down_weight)


def solution(mesh):
    n = mesh.shape["gx"]
    return jax.shard_map(
        functools.partial(local, n),
        mesh=mesh,
        in_specs=(P(("groups", "gx"), "gy"), P("gx", "gy"), P("gx", "gy"), P("gx", "gy")),
        out_specs=P(("groups", "gx"), "gy"),
        check_vma=False,
    )
```

time: 286 us -> 44.1 us (0.15)
  waiting for transfers between devices: 174 us -> 0 us
  blocking collectives: 67.3 us -> 0 us
  Pallas kernels: 0 us -> 42.6 us
  matrix products: 22.5 us -> 0 us
  between operations: 14.2 us -> 0.01 us
  local copies, waits for them, and re-layouts: 4.81 us -> 1.39 us
    unnamed x12 -> x0, waiting for transfers between devices: 174 us -> none
    all_gather x4 -> x0, blocking collectives: 67.3 us -> none  [the longest x2 63.6 us: local(): block_rows = lax.all_gather(stream, 'gx', axis=0, tiled=True)]
    pallas_call x0 -> x1, Pallas kernels: none -> 42.6 us  [local(): pl.pallas_call(functools.partial(kernel, n), out_shape=jax.ShapeDtypeStru...]
    unnamed x4 -> x0, matrix products: 15.3 us -> none
    dot_general x2 -> x0, matrix products: 7.2 us -> none  [local(): jnp.dot(hidden, down_weight, preferred_element_type=jnp.float32)]
    unnamed x13 -> x1, local copies, waits for them, and re-layouts: 4.74 us -> 1.39 us
  transfers between devices with their start and end apart: 6 -> 0, of which waited for: 6 -> 0; matrix products, arithmetic and copies ran while one was open for 4% -> 0% of each run, Pallas kernels for 0% -> 0%
where the time goes in v1:
time: 44.1 us; the launch traced here: 44 us
  Pallas kernels  42.6 us (97%)
  local copies, waits for them, and re-layouts  1.39 us (3%)
    pallas_call x1, Pallas kernels, local(): pl.pallas_call(functools.partial(kernel, n), out_shape=jax.ShapeDtypeStru...  42.6 us
    unnamed x1, local copies, waits for them, and re-layouts  1.39 us

profile of v1, /device:TPU:0, one launch (start us, length us, event | category | flops | bytes accessed | tf_op | source)
XLA Modules:
  0.0 44.0 jit_solution(15206994640996494573)
XLA Ops:
  0.0 42.6 %shard_map.46 = bf16[4,4096]{1,0:T(4,128)(2,1)} custom-call(bf16[4,4096]{1,0:T(4,128)(2,1)} %tokens.1, bf16[448,4096]{1,0:T(8,128)(2,1)} %wg_hbm.1, bf16[448,4096]{1,0:T(8,128)(2,1)} %wu_hbm.1, bf16[448,4096]{1,0:T(8,128)(2,1)} %wd_hbm.1), custom_call_target="tpu_custom_call" | custom-call | flops 704643072 | bytes 11010048 | tf_op jit(solution)/shard_map/pallas_call | solution.py:135
  42.6 1.4 %copy.6 = bf16[4,4096]{1,0:T(4,128)(2,1)} copy(bf16[4,4096]{1,0:T(4,128)(2,1)} %shard_map.46) | data formatting | bytes 65536

commit v2 on v1

v2 whole, which is shorter than its diff:
```python
import functools

import jax
import jax.numpy as jnp
from jax import lax
from jax.experimental import pallas as pl
from jax.experimental.pallas import tpu as pltpu
from jax.sharding import PartitionSpec as P

LAYERS = 2
CHUNKS = 4
SKEW = 2.5
MESH = pl.DeviceIdType.MESH
F32 = jnp.float32
BF16 = jnp.bfloat16
NT = (((1,), (1,)), ((), ()))


def kernel(n, nx, tokens, wg_hbm, wu_hbm, wd_hbm, out,
           wg, wu, wd, ag, snd, xin, mid, zin, part, part_in,
           w_sem, tok_sem, agz_send, agz_recv, agx_send, agx_recv,
           rsx_send, rsx_recv, rsz_send, rsz_recv, gy_send, gy_recv):
    nz = n // nx
    me = lax.axis_index("gx")
    my_x, my_z = lax.rem(me, nx), lax.div(me, nx)
    other = 1 - lax.axis_index("gy")
    r, d = tokens.shape
    kc = d // CHUNKS
    rows = n * r

    def cols(c):
        return pl.ds(c * kc, kc)

    def at(x, z):
        return {"gx": z * nx + x}

    def z_peers(body):
        def step(i, carry):
            body(lax.rem(my_z + i, nz))
            return carry
        lax.fori_loop(1, nz, step, 0, unroll=nz <= 4)

    def x_peers(body):
        def step(i, carry):
            body(lax.rem(my_x + i, nx))
            return carry
        lax.fori_loop(1, nx, step, 0, unroll=nx <= 4)

    def arrived(buf, sem):
        pltpu.make_async_copy(buf, buf, sem).wait()

    own = [pltpu.make_async_copy(tokens.at[:, cols(c)], ag.at[0, c, my_x, my_z], tok_sem.at[c])
           for c in range(CHUNKS)]
    for t in own:
        t.start()
    weights = {}
    for k, (h, v) in enumerate(((wg_hbm, wg), (wu_hbm, wu), (wd_hbm, wd))):
        for c in range(CHUNKS):
            weights[k, c] = pltpu.make_async_copy(h.at[:, cols(c)], v.at[c], w_sem.at[k, c])
    for c in range(CHUNKS):
        weights[0, c].start()
        weights[1, c].start()
    for c in range(CHUNKS):
        weights[2, c].start()

    barrier = pltpu.get_barrier_semaphore()
    z_peers(lambda z: pl.semaphore_signal(barrier, inc=1, device_id=at(my_x, z), device_id_type=MESH))
    x_peers(lambda x: pl.semaphore_signal(barrier, inc=1, device_id=at(x, my_z), device_id_type=MESH))
    pl.semaphore_signal(barrier, inc=1, device_id={"gy": other}, device_id_type=MESH)
    for t in own:
        t.wait()
    pl.semaphore_wait(barrier, nz + nx - 1)

    def gather_z(l, c):
        z_peers(lambda z: pltpu.make_async_remote_copy(
            src_ref=ag.at[l, c, my_x, my_z], dst_ref=ag.at[l, c, my_x, my_z],
            send_sem=agz_send.at[l], recv_sem=agz_recv.at[l, c],
            device_id=at(my_x, z), device_id_type=MESH).start())

    def gather_x(l, c):
        arrived(ag.at[l, c, 0, pl.ds(0, nz - 1)], agz_recv.at[l, c])
        x_peers(lambda x: pltpu.make_async_remote_copy(
            src_ref=ag.at[l, c, my_x], dst_ref=ag.at[l, c, my_x],
            send_sem=agx_send.at[l], recv_sem=agx_recv.at[l, c],
            device_id=at(x, my_z), device_id_type=MESH).start())

    def gate_up(l, c, acc):
        if l == 0:
            weights[0, c].wait()
            weights[1, c].wait()
        arrived(ag.at[l, c, pl.ds(0, nx - 1)], agx_recv.at[l, c])
        x = ag[l, c].astype(F32).reshape(rows, kc).astype(BF16)
        for k, w in enumerate((wg, wu)):
            v = lax.dot_general(x, w[c], NT, preferred_element_type=F32)
            acc[k] = v if acc[k] is None else acc[k] + v

    def exchange(l, acc):
        part[l, 0] = acc[0]
        part[l, 1] = acc[1]
        swap = pltpu.make_async_remote_copy(
            src_ref=part.at[l], dst_ref=part_in.at[l],
            send_sem=gy_send.at[l], recv_sem=gy_recv.at[l],
            device_id={"gy": other}, device_id_type=MESH)
        swap.start()
        if l == 0:
            for c in range(CHUNKS):
                weights[2, c].wait()
        swap.wait()
        gate = part[l, 0] + part_in[l, 0]
        up = part[l, 1] + part_in[l, 1]
        return (jax.nn.silu(gate) * up).astype(BF16)

    def down(l, c, hidden):
        p = jnp.dot(hidden, wd[c], preferred_element_type=F32)
        snd[l, c] = p.astype(BF16).reshape(nx, nz * r, kc)
        x_peers(lambda x: pltpu.make_async_remote_copy(
            src_ref=snd.at[l, c, x], dst_ref=xin.at[l, c, my_x],
            send_sem=rsx_send.at[l], recv_sem=rsx_recv.at[l, c],
            device_id=at(x, my_z), device_id_type=MESH).start())
        xin[l, c, my_x] = snd[l, c, my_x]

    def scatter_z(l, c):
        arrived(xin.at[l, c, pl.ds(0, nx - 1)], rsx_recv.at[l, c])
        total = jnp.sum(xin[l, c].astype(F32), axis=0)
        mid[l, c] = total.reshape(nz, r, kc).astype(BF16)
        z_peers(lambda z: pltpu.make_async_remote_copy(
            src_ref=mid.at[l, c, z], dst_ref=zin.at[l, c, my_z],
            send_sem=rsz_send.at[l], recv_sem=rsz_recv.at[l, c],
            device_id=at(my_x, z), device_id_type=MESH).start())
        zin[l, c, my_z] = mid[l, c, my_z]

    def update(l, c):
        arrived(zin.at[l, c, pl.ds(0, nz - 1)], rsz_recv.at[l, c])
        summed = jnp.sum(zin[l, c].astype(F32), axis=0)
        stream = (ag[l, c, my_x, my_z].astype(F32) + summed).astype(BF16)
        if l + 1 < LAYERS:
            ag[l + 1, c, my_x, my_z] = stream
            gather_z(l + 1, c)
        else:
            out[:, cols(c)] = stream

    for c in range(CHUNKS):
        gather_z(0, c)
    for l in range(LAYERS + 1):
        stages = []
        if l > 0:
            stages += [lambda c: scatter_z(l - 1, c), lambda c: update(l - 1, c)]
            for c in range(CHUNKS):
                down(l - 1, c, hidden)
        if l < LAYERS:
            acc = [None, None]
            stages += [lambda c: gather_x(l, c), lambda c: gate_up(l, c, acc)]
        order = sorted((k * SKEW + c, -k, k, c) for k in range(len(stages)) for c in range(CHUNKS))
        for _, _, k, c in order:
            stages[k](c)
        if l < LAYERS:
            hidden = exchange(l, acc)
    for l in range(LAYERS):
        arrived(ag.at[l, :, 0, pl.ds(0, nz - 1)], agz_send.at[l])
        arrived(ag.at[l, :, pl.ds(0, nx - 1)], agx_send.at[l])
        arrived(snd.at[l, :, pl.ds(0, nx - 1)], rsx_send.at[l])
        arrived(mid.at[l, :, pl.ds(0, nz - 1)], rsz_send.at[l])


def columns_of(n):
    nx = 2
    while nx ** 3 < n:
        nx *= 2
    return nx


def local(n, tokens, gate_weight, up_weight, down_weight):
    r, d = tokens.shape
    units = gate_weight.shape[0]
    rows = n * r
    nx = columns_of(n)
    nz = n // nx
    kc = d // CHUNKS
    flops = 2 * LAYERS * 3 * rows * units * d
    return pl.pallas_call(
        functools.partial(kernel, n, nx),
        out_shape=jax.ShapeDtypeStruct((r, d), BF16),
        in_specs=[pl.BlockSpec(memory_space=pl.ANY)] * 4,
        out_specs=pl.BlockSpec(memory_space=pltpu.VMEM),
        scratch_shapes=[
            pltpu.VMEM((CHUNKS, units, kc), BF16),
            pltpu.VMEM((CHUNKS, units, kc), BF16),
            pltpu.VMEM((CHUNKS, units, kc), BF16),
            pltpu.VMEM((LAYERS, CHUNKS, nx, nz, r, kc), BF16),
            pltpu.VMEM((LAYERS, CHUNKS, nx, nz * r, kc), BF16),
            pltpu.VMEM((LAYERS, CHUNKS, nx, nz * r, kc), BF16),
            pltpu.VMEM((LAYERS, CHUNKS, nz, r, kc), BF16),
            pltpu.VMEM((LAYERS, CHUNKS, nz, r, kc), BF16),
            pltpu.VMEM((LAYERS, 2, rows, units), F32),
            pltpu.VMEM((LAYERS, 2, rows, units), F32),
            pltpu.SemaphoreType.DMA((3, CHUNKS)),
            pltpu.SemaphoreType.DMA((CHUNKS,)),
            pltpu.SemaphoreType.DMA((LAYERS,)),
            pltpu.SemaphoreType.DMA((LAYERS, CHUNKS)),
            pltpu.SemaphoreType.DMA((LAYERS,)),
            pltpu.SemaphoreType.DMA((LAYERS, CHUNKS)),
            pltpu.SemaphoreType.DMA((LAYERS,)),
            pltpu.SemaphoreType.DMA((LAYERS, CHUNKS)),
            pltpu.SemaphoreType.DMA((LAYERS,)),
            pltpu.SemaphoreType.DMA((LAYERS, CHUNKS)),
            pltpu.SemaphoreType.DMA((LAYERS,)),
            pltpu.SemaphoreType.DMA((LAYERS,)),
        ],
        compiler_params=pltpu.CompilerParams(
            collective_id=0, has_side_effects=True, vmem_limit_bytes=56 * 1024 * 1024),
        cost_estimate=pl.CostEstimate(
            flops=flops, bytes_accessed=3 * units * d * 2, transcendentals=LAYERS * rows * units),
    )(tokens, gate_weight, up_weight, down_weight)


def solution(mesh):
    n = mesh.shape["gx"]
    return jax.shard_map(
        functools.partial(local, n),
        mesh=mesh,
        in_specs=(P(("groups", "gx"), "gy"), P("gx", "gy"), P("gx", "gy"), P("gx", "gy")),
        out_specs=P(("groups", "gx"), "gy"),
        check_vma=False,
    )
```

time: 44.1 us -> 50.9 us (1.15)
  Pallas kernels: 42.6 us -> 49.3 us
    pallas_call x1, Pallas kernels: 42.6 us -> 49.3 us  [local(): pl.pallas_call(functools.partial(kernel, n, nx), out_shape=jax.ShapeDtype...]
where the time goes in v2:
time: 50.9 us; the launch traced here: 50.7 us
  Pallas kernels  49.3 us (97%)
  local copies, waits for them, and re-layouts  1.39 us (3%)
    pallas_call x1, Pallas kernels, local(): pl.pallas_call(functools.partial(kernel, n, nx), out_shape=jax.ShapeDtype...  49.3 us
    unnamed x1, local copies, waits for them, and re-layouts  1.39 us

profile of v2, /device:TPU:0, one launch (start us, length us, event | category | flops | bytes accessed | tf_op | source)
XLA Modules:
  0.0 50.7 jit_solution(13099062840050354340)
XLA Ops:
  0.0 49.3 %shard_map.46 = bf16[4,4096]{1,0:T(4,128)(2,1)} custom-call(bf16[4,4096]{1,0:T(4,128)(2,1)} %tokens.1, bf16[448,4096]{1,0:T(8,128)(2,1)} %wg_hbm.1, bf16[448,4096]{1,0:T(8,128)(2,1)} %wu_hbm.1, bf16[448,4096]{1,0:T(8,128)(2,1)} %wd_hbm.1), custom_call_target="tpu_custom_call" | custom-call | flops 704643072 | bytes 11010048 | tf_op jit(solution)/shard_map/pallas_call | solution.py:180
  49.3 1.4 %copy.6 = bf16[4,4096]{1,0:T(4,128)(2,1)} copy(bf16[4,4096]{1,0:T(4,128)(2,1)} %shard_map.46) | data formatting | bytes 65536

commit v3 on v1

--- a/solution.py
+++ b/solution.py
@@ -56,24 +56,39 @@
         t.wait()
     pl.semaphore_wait(barrier, n)
 
+    def flipped(k):
+        peer, bit = me, 1
+        while bit <= k:
+            if k & bit:
+                peer = peer + bit - 2 * bit * lax.rem(lax.div(me, bit), 2)
+            bit *= 2
+        return peer
+
+    def peers(body):
+        if n <= 8:
+            for k in range(n - 1, 0, -1):
+                body(flipped(k))
+        else:
+            def step(i, carry):
+                body(lax.rem(me + i, n))
+                return carry
+            lax.fori_loop(1, n, step, 0)
+
     def send_ag(l, c):
-        def body(i, carry):
+        def body(peer):
             pltpu.make_async_remote_copy(
                 src_ref=ag.at[l, c, me], dst_ref=ag.at[l, c, me],
                 send_sem=ag_send.at[l], recv_sem=ag_recv.at[l, c],
-                device_id={"gx": lax.rem(me + i, n)}, device_id_type=MESH).start()
-            return carry
-        lax.fori_loop(1, n, body, 0, unroll=unroll)
+                device_id={"gx": peer}, device_id_type=MESH).start()
+        peers(body)
 
     def send_rs(l, c):
-        def body(i, carry):
-            peer = lax.rem(me + i, n)
+        def body(peer):
             pltpu.make_async_remote_copy(
                 src_ref=snd.at[l, c, peer], dst_ref=rcv.at[l, c, me],
                 send_sem=rs_send.at[l], recv_sem=rs_recv.at[l, c],
                 device_id={"gx": peer}, device_id_type=MESH).start()
-            return carry
-        lax.fori_loop(1, n, body, 0, unroll=unroll)
+        peers(body)
 
     def arrived(buf, sem):
         pltpu.make_async_copy(buf, buf, sem).wait()

time: 44.1 us -> 42.8 us (0.971)
  Pallas kernels: 42.6 us -> 41.2 us
    pallas_call x1, Pallas kernels: 42.6 us -> 41.2 us  [local(): pl.pallas_call(functools.partial(kernel, n), out_shape=jax.ShapeDtypeStru...]
where the time goes in v3:
time: 42.8 us; the launch traced here: 42.6 us
  Pallas kernels  41.2 us (96%)
  local copies, waits for them, and re-layouts  1.39 us (3%)
    pallas_call x1, Pallas kernels, local(): pl.pallas_call(functools.partial(kernel, n), out_shape=jax.ShapeDtypeStru...  41.2 us
    unnamed x1, local copies, waits for them, and re-layouts  1.39 us

profile of v3, /device:TPU:0, one launch (start us, length us, event | category | flops | bytes accessed | tf_op | source)
XLA Modules:
  0.0 42.6 jit_solution(14366461288226024879)
XLA Ops:
  0.0 41.2 %shard_map.46 = bf16[4,4096]{1,0:T(4,128)(2,1)} custom-call(bf16[4,4096]{1,0:T(4,128)(2,1)} %tokens.1, bf16[448,4096]{1,0:T(8,128)(2,1)} %wg_hbm.1, bf16[448,4096]{1,0:T(8,128)(2,1)} %wu_hbm.1, bf16[448,4096]{1,0:T(8,128)(2,1)} %wd_hbm.1), custom_call_target="tpu_custom_call" | custom-call | flops 704643072 | bytes 11010048 | tf_op jit(solution)/shard_map/pallas_call | solution.py:150
  41.2 1.4 %copy.6 = bf16[4,4096]{1,0:T(4,128)(2,1)} copy(bf16[4,4096]{1,0:T(4,128)(2,1)} %shard_map.46) | data formatting | bytes 65536

commit v4 on v1

--- a/solution.py
+++ b/solution.py
@@ -28,6 +28,28 @@
     def cols(c):
         return pl.ds(c * kc, kc)
 
+    def flipped(k):
+        peer, bit = me, 1
+        while bit <= k:
+            if k & bit:
+                peer = peer + bit - 2 * bit * lax.rem(lax.div(me, bit), 2)
+            bit *= 2
+        return peer
+
+    def peers(body):
+        if n <= 8:
+            for k in range(n - 1, 0, -1):
+                body(flipped(k))
+        else:
+            def step(i, carry):
+                body(lax.rem(me + i, n))
+                return carry
+            lax.fori_loop(1, n, step, 0)
+
+    barrier = pltpu.get_barrier_semaphore()
+    peers(lambda peer: pl.semaphore_signal(
+        barrier, inc=1, device_id={"gx": peer}, device_id_type=MESH))
+    pl.semaphore_signal(barrier, inc=1, device_id={"gy": other}, device_id_type=MESH)
     loads = []
     for c in range(CHUNKS):
         t = pltpu.make_async_copy(tokens.at[:, cols(c)], ag.at[0, c, me], tok_sem.at[c])
@@ -43,37 +65,25 @@
     for c in range(CHUNKS):
         weights[2, c].start()
 
-    barrier = pltpu.get_barrier_semaphore()
-
-    def greet(i, carry):
-        pl.semaphore_signal(barrier, inc=1, device_id={"gx": lax.rem(me + i, n)}, device_id_type=MESH)
-        return carry
-
-    unroll = n <= 8
-    lax.fori_loop(1, n, greet, 0, unroll=unroll)
-    pl.semaphore_signal(barrier, inc=1, device_id={"gy": other}, device_id_type=MESH)
     for t in loads:
         t.wait()
     pl.semaphore_wait(barrier, n)
 
     def send_ag(l, c):
-        def body(i, carry):
+        def body(peer):
             pltpu.make_async_remote_copy(
                 src_ref=ag.at[l, c, me], dst_ref=ag.at[l, c, me],
                 send_sem=ag_send.at[l], recv_sem=ag_recv.at[l, c],
-                device_id={"gx": lax.rem(me + i, n)}, device_id_type=MESH).start()
-            return carry
-        lax.fori_loop(1, n, body, 0, unroll=unroll)
+                device_id={"gx": peer}, device_id_type=MESH).start()
+        peers(body)
 
     def send_rs(l, c):
-        def body(i, carry):
-            peer = lax.rem(me + i, n)
+        def body(peer):
             pltpu.make_async_remote_copy(
                 src_ref=snd.at[l, c, peer], dst_ref=rcv.at[l, c, me],
                 send_sem=rs_send.at[l], recv_sem=rs_recv.at[l, c],
                 device_id={"gx": peer}, device_id_type=MESH).start()
-            return carry
-        lax.fori_loop(1, n, body, 0, unroll=unroll)
+        peers(body)
 
     def arrived(buf, sem):
         pltpu.make_async_copy(buf, buf, sem).wait()

time: 44.1 us -> 42.8 us (0.971)
  Pallas kernels: 42.6 us -> 41.2 us
    pallas_call x1, Pallas kernels: 42.6 us -> 41.2 us  [local(): pl.pallas_call(functools.partial(kernel, n), out_shape=jax.ShapeDtypeStru...]
where the time goes in v4:
time: 42.8 us; the launch traced here: 42.6 us
  Pallas kernels  41.2 us (96%)
  local copies, waits for them, and re-layouts  1.39 us (3%)
    pallas_call x1, Pallas kernels, local(): pl.pallas_call(functools.partial(kernel, n), out_shape=jax.ShapeDtypeStru...  41.2 us
    unnamed x1, local copies, waits for them, and re-layouts  1.39 us

profile of v4, /device:TPU:0, one launch (start us, length us, event | category | flops | bytes accessed | tf_op | source)
XLA Modules:
  0.0 42.6 jit_solution(11559584871267008140)
XLA Ops:
  0.0 41.2 %shard_map.46 = bf16[4,4096]{1,0:T(4,128)(2,1)} custom-call(bf16[4,4096]{1,0:T(4,128)(2,1)} %tokens.1, bf16[448,4096]{1,0:T(8,128)(2,1)} %wg_hbm.1, bf16[448,4096]{1,0:T(8,128)(2,1)} %wu_hbm.1, bf16[448,4096]{1,0:T(8,128)(2,1)} %wd_hbm.1), custom_call_target="tpu_custom_call" | custom-call | flops 704643072 | bytes 11010048 | tf_op jit(solution)/shard_map/pallas_call | solution.py:145
  41.2 1.4 %copy.6 = bf16[4,4096]{1,0:T(4,128)(2,1)} copy(bf16[4,4096]{1,0:T(4,128)(2,1)} %shard_map.46) | data formatting | bytes 65536
